TPU v7x, 32 devices: a whole 2x2x4 slice. The times are simulated.
32 devices in a mesh: groups: 2 (over x), blk: 16 (over z, y, core).
Axes of the slice: x: 2, y: 2, z: 4, core: 2. Of those that a mesh axis runs over, the one named last changes fastest.
Arguments:
- hidden: bfloat16 [12288, 5120], P(('groups', 'blk')), parts along dimension 0, may hold values from -6 to 6
- norm_gain: float32 [5120], replicated, may hold values from 0.5 to 1.5
- q_weight: bfloat16 [5120, 2560], P('blk'), may hold values from -0.078125 to 0.078125
- q_bias: float32 [2560], replicated, may hold values from -5 to 5
- kv_store: bfloat16 [128, 2, 512, 512], P(('groups', 'blk')), parts along dimension 0, may hold values from -620 to 620
- block_home: int32 [128], P('groups'), parts along dimension 0, may hold values from 0 to 63, as said below
- need_ids: int32 [64, 2], P(('groups', 'blk')), parts along dimension 0, may hold values from 0 to 63, as said below
- hole_pos: int32 [64], P(('groups', 'blk')), parts along dimension 0, may hold values from 0 to 32767, as said below
- fill_len: int32 [64], P(('groups', 'blk')), parts along dimension 0, may hold values from 48 to 192
Outputs:
- attended: bfloat16 [12288, 2560], P(('groups', 'blk')), parts along dimension 0
There are 2 independent parts, one for each index of `groups`. A program takes and returns all parts, laid end to end along the dimension named above; an argument that names none is the same for every part. Nothing has to cross between parts.
Inputs may be any that keep to these rules, and one draw needn't show every extreme that they name: block_home is a permutation; block b is kept by device block_home[b] // 4 of blk. `need_ids`: the 4 blocks listed by the candidates of one device of blk are all different and are kept by different devices, each at most 2 places away from it along blk, counted around the loop. The span from hole_pos to hole_pos + fill_len - 1 lies inside the first block that the candidate lists.
All inputs are finite; a program needn't handle non-finite values.
Results may differ from a plain program's by a relative error of at most 0.0035.
The roundings to bfloat16 on the way count: a program that leaves them out, or rounds other values in their place, can miss the bound.
Values may be sent and summed in bfloat16 or wider, within the bound.
A program may use at most 128 MiB of HBM per device.

v0:
```python
import math
import jax
import jax.numpy as jnp
from jax import lax
from jax.sharding import PartitionSpec as P

HEAD_SIZE = 128
QUERY_HEADS = 20
KEY_HEADS = 4
BLOCK_TOKENS = 512
BLOCKS_NEEDED = 2
REACH = 2


def passed_along(block, axis, distance):
    devices = range(lax.axis_size(axis))
    route = [((i - distance) % len(devices), i) for i in devices]
    return lax.ppermute(block, axis, route)


def rms_normed(hidden, norm_gain):
    widened = hidden.astype(jnp.float32)
    scale_inv = lax.rsqrt(jnp.mean(widened * widened, axis=-1, keepdims=True) + 1e-06)
    return (widened * scale_inv * norm_gain).astype(jnp.bfloat16)


def attend_single(packed):
    candidate_query_rows, sketch_blocks, block_ids, hole_start, fill_rows = packed
    count_of_rows = candidate_query_rows.shape[0]
    block_key_rows = sketch_blocks[:, 0].reshape(BLOCKS_NEEDED * BLOCK_TOKENS, KEY_HEADS, HEAD_SIZE)
    block_value_rows = sketch_blocks[:, 1].reshape(
        BLOCKS_NEEDED * BLOCK_TOKENS, KEY_HEADS, HEAD_SIZE
    )
    query_matrix = candidate_query_rows.reshape(
        count_of_rows, KEY_HEADS, QUERY_HEADS // KEY_HEADS, HEAD_SIZE
    )
    scores = jnp.einsum(
        "rkgd,tkd->rkgt", query_matrix, block_key_rows, preferred_element_type=jnp.float32
    ) / math.sqrt(HEAD_SIZE)
    position = (
        block_ids[:, None] * BLOCK_TOKENS + jnp.arange(BLOCK_TOKENS, dtype=jnp.int32)[None, :]
    ).reshape(BLOCKS_NEEDED * BLOCK_TOKENS)
    masked = (position >= hole_start) & (position < hole_start + fill_rows)
    scores = jnp.where(masked[None, None, None, :], jnp.float32(-1e30), scores)
    row_max = jnp.max(scores, axis=-1, keepdims=True)
    exponent = jnp.exp(scores - row_max)
    denominator = jnp.sum(exponent, axis=-1)
    weights = exponent.astype(jnp.bfloat16)
    attended = (
        jnp.einsum("rkgt,tkd->rkgd", weights, block_value_rows, preferred_element_type=jnp.float32)
        / denominator[..., None]
    )
    attended = attended.reshape(count_of_rows, QUERY_HEADS * HEAD_SIZE)
    live_rows = jnp.arange(count_of_rows, dtype=jnp.int32) < fill_rows
    return jnp.where(live_rows[:, None], attended, jnp.float32(0.0)).astype(jnp.bfloat16)


def attend_all(query, sketch_blocks, block_lists, hole_starts, fill_rows):
    cand_count = block_lists.shape[0]
    count_of_rows = query.shape[0] // cand_count
    shaped = query.reshape(cand_count, count_of_rows, QUERY_HEADS * HEAD_SIZE)
    results = lax.map(attend_single, (shaped, sketch_blocks, block_lists, hole_starts, fill_rows))
    return results.reshape(cand_count * count_of_rows, QUERY_HEADS * HEAD_SIZE)


def shards(hidden, norm_gain, q_weight, q_bias, kv_store, block_home, need_ids, hole_pos, fill_len):
    normed = rms_normed(hidden, norm_gain)
    whole_weight = lax.all_gather(q_weight, "blk", axis=0, tiled=True)
    projected = jnp.dot(normed, whole_weight, preferred_element_type=jnp.float32)
    query = (projected + q_bias).astype(jnp.bfloat16)
    device_count = lax.axis_size("blk")
    myself = lax.axis_index("blk")
    local_count = kv_store.shape[0]
    empty_block = jnp.zeros(kv_store.shape[1:], kv_store.dtype)

    def select_block(block_lists):
        stored_at = block_home[block_lists.reshape(-1)]
        owned_here = stored_at // local_count == myself
        slot_index = jnp.sum(jnp.where(owned_here, stored_at % local_count, 0))
        has_block = jnp.any(owned_here)
        chosen = lax.dynamic_index_in_dim(kv_store, slot_index, 0, keepdims=False)
        return jnp.where(has_block, chosen, empty_block)

    incoming = []
    for offset in range(-REACH, REACH + 1):
        if offset == 0:
            incoming.append(select_block(need_ids))
        else:
            asked = passed_along(need_ids, "blk", -offset)
            incoming.append(passed_along(select_block(asked), "blk", offset))
    arrived = jnp.stack(incoming, axis=0)
    owners = block_home[need_ids] // local_count
    slot_of_entry = jnp.remainder(myself - owners + REACH, device_count)
    sketch_blocks = jnp.take(arrived, slot_of_entry, axis=0)
    return attend_all(query, sketch_blocks, need_ids, hole_pos, fill_len)


def solution(mesh):
    placed = (
        P(("groups", "blk"), None),
        P(),
        P("blk", None),
        P(),
        P(("groups", "blk"), None, None, None),
        P("groups"),
        P(("groups", "blk"), None),
        P(("groups", "blk")),
        P(("groups", "blk")),
    )
    return jax.shard_map(
        shards, mesh=mesh, in_specs=placed, out_specs=P(("groups", "blk"), None), check_vma=False
    )
```

profile of v0, /device:TPU:0, one launch (start us, length us, event | category | flops | bytes accessed | tf_op | source)
XLA Modules:
  0.0 285.8 jit_solution(10790405811085733742)
XLA Ops:
  7.8 2.6 collective-permute-start
  10.3 4.1 %collective-permute-start.4 = (s32[2,2]{1,0:T(2,128)}, s32[2,2]{1,0:T(2,128)S(1)}, u32[]{:S(2)}, u32[]{:S(2)}) collective-permute-start(s32[2,2]{1,0:T(2,128)} %param.17), channel_id=1, source_target_pairs={{1,0},{2,1},{3,2},{4,3},{5,4},{6,5},{7,6},{8,7},{9,8},{10,9},{11,1... | collective-permute-start | bytes 56 | tf_op jit(solution)/shard_map/ppermute | solution.py:18
  29.1 4.0 %select_bitcast_fusion.2 = (bf16[2,512,512]{2,1,0:T(8,128)(2,1)S(1)}, bf16[2,512,512]{2,1,0:T(8,128)(2,1)}) fusion(bf16[4,2,512,512]{3,2,1,0:T(8,128)(2,1)} %param.15, s32[]{:T(128)S(6)} %select_n.257, pred[]{:T(512)} %get-tuple-element.77, s32[]{:T(128)S(6)} %select_n.249, pred[]{:T(512)} %get-tuple-element.92), kind=kLoop, calls=%fused_computation.48 | loop fusion | flops 1048576 | bytes 4194314 | tf_op jit(solution)/shard_map/jit(_where)/select_n | solution.py:82
  33.1 2.8 collective-permute-start.1
  43.1 38.2 %collective-permute-done.1 = bf16[2,512,512]{2,1,0:T(8,128)(2,1)S(1)} collective-permute-done((bf16[2,512,512]{2,1,0:T(8,128)(2,1)}, bf16[2,512,512]{2,1,0:T(8,128)(2,1)S(1)}, u32[]{:S(2)}, u32[]{:S(2)}) %collective-permute-start.1) | collective-permute-done | bytes 1048608 | tf_op jit(solution)/shard_map/ppermute | solution.py:18
  81.3 33.3 %collective-permute-done.3 = bf16[2,512,512]{2,1,0:T(8,128)(2,1)S(1)} collective-permute-done((bf16[2,512,512]{2,1,0:T(8,128)(2,1)S(1)}, bf16[2,512,512]{2,1,0:T(8,128)(2,1)S(1)}, u32[]{:S(2)}, u32[]{:S(2)}) %collective-permute-start.3) | collective-permute-done | bytes 1048608 | tf_op jit(solution)/shard_map/ppermute | solution.py:18
  114.7 2.4 select_bitcast_fusion
  117.1 2.4 copy-done.4
  120.1 1.2 collective-permute-start.7
  121.4 3.0 %fusion.15 = f32[384]{0:T(512)S(1)} fusion(bf16[384,5120]{1,0:T(8,128)(2,1)} %param.11), kind=kLoop, calls=%fused_computation.33 | loop fusion | flops 5897856 | bytes 3933696 | tf_op jit(solution)/shard_map/reduce_sum | solution.py:23
  124.5 45.0 %collective-permute-done.5 = bf16[2,512,512]{2,1,0:T(8,128)(2,1)S(1)} collective-permute-done((bf16[2,512,512]{2,1,0:T(8,128)(2,1)S(1)}, bf16[2,512,512]{2,1,0:T(8,128)(2,1)S(1)}, u32[]{:S(2)}, u32[]{:S(2)}) %collective-permute-start.5) | collective-permute-done | bytes 1048608 | tf_op jit(solution)/shard_map/ppermute | solution.py:18
  172.3 5.3 %gather_fusion.6 = bf16[4,2,512,512]{3,2,1,0:T(8,128)(2,1)} fusion(bf16[5,2,512,512]{3,2,1,0:T(8,128)(2,1)} %bitcast_dynamic-update-slice_fusion, s32[1024]{0:T(1024)S(1)} %pad_clamp_fusion), kind=kCustom, calls=%fused_computation.6 | custom fusion | bytes 8388624 | tf_op jit(solution)/shard_map/jit(_take)/gather | solution.py:94
  177.6 4.7 %broadcast_select_fusion = bf16[2,2,2,512,512]{4,3,2,1,0:T(8,128)(2,1)} fusion(bf16[2,2,2,512,512]{4,3,2,1,0:T(8,128)(2,1)} %bitcast.95, pred[2,2]{1,0:T(4,128)(4,1)S(1)} %compare_and_fusion.1), kind=kLoop, calls=%fused_computation.38 | loop fusion | flops 2097152 | bytes 8388612 | tf_op jit(solution)/shard_map/jit(_take)/select_n | solution.py:94
  182.3 30.0 %all-gather.2.cloned.1.call-done = bf16[5120,2560]{1,0:T(8,128)(2,1)} async-done(((bf16[320,2560]{1,0:T(8,128)(2,1)}), bf16[5120,2560]{1,0:T(8,128)(2,1)}) %all-gather.2.cloned.1.call-update) | async-done | bytes 26214416 | tf_op jit(solution)/shard_map/all_gather | solution.py:68
  212.3 17.5 %fusion.18 = bf16[384,2560]{1,0:T(8,128)(2,1)} fusion(bf16[5120,2560]{1,0:T(8,128)(2,1)} %all-gather.2.cloned.1.call-done, bf16[384,5120]{1,0:T(8,128)(2,1)} %param.11, f32[5120]{0:T(1024)S(1)} %copy-done.6, f32[384]{0:T(512)S(1)} %add_rsqrt_fusion, f32[2560]{0:T(1024)S(1)} %copy-done.7), kind=kOutput, calls=%fused_computation.37 | convolution fusion | flops 10076160000 | bytes 32144896 | tf_op jit(solution)/shard_map/dot_general | solution.py:69
  229.8 48.5 %while.10 = (s32[]{:T(128)}, bf16[2,192,2560]{2,1,0:T(8,128)(2,1)}, s32[2]{0:T(128)S(1)}, bf16[2,2,2,512,512]{4,3,2,1,0:T(8,128)(2,1)}, s32[2,2]{1,0:T(2,128)S(1...) while((s32[]{:T(128)}, bf16[2,192,2560]{2,1,0:T(8,128)(2,1)}, s32[2]{0:T(128)S(1)}, ...), condition=%wide.region_14.15_spmd, body=%wide.region_11.14_spmd.sunk | while | flops 2057990912 | bytes 79906376 | solution.py:62
  233.5 1.3 constant_dynamic-slice_fusion.7
  235.3 1.7 copy_bitcast_fusion.2
  237.1 1.2 fusion.47
  238.3 1.3 squeeze.29
  239.6 1.1 squeeze.30
  240.8 2.9 %bitcast_reduce_fusion.2 = (f32[192,4,5]{0,2,1:T(8,128)S(1)}, f32[4,1024,192,5]{1,2,3,0:T(8,128)S(1)}) fusion(pred[1024]{0:T(1024)(128)(4,1)S(1)} %and.179, bf16[192,4,5,128]{0,3,2,1:T(8,128)(2,1)S(1)} %bitcast.91, bf16[1024,4,128,1]{2,1,0,3:T(4,128)(2,1)S(1)} %bitcast.93), kind=kOutput, calls=%fused_computation.8.clone.1 | convolution fusion | flops 1018425600 | bytes 17776640 | tf_op jit(solution)/shard_map/while/body/eval_jaxpr/rkgd,tkd->rkgt/dot_general | solution.py:37
  243.7 3.9 %fusion.48 = f32[192,4,5]{0,2,1:T(8,128)S(1)} fusion(f32[4,1024,192,5]{1,2,3,0:T(8,128)S(1)} %get-tuple-element.144, f32[192,4,5]{0,2,1:T(8,128)S(1)} %get-tuple-element.145, pred[1024]{0:T(1024)(128)(4,1)S(1)} %and.179), kind=kLoop, calls=%fused_computation.11.clone.1 | loop fusion | flops 15724800 | bytes 15760384 | tf_op jit(solution)/shard_map/while/body/eval_jaxpr/reduce_sum | solution.py:47
  247.7 3.9 %bitcast_divide_fusion.2 = bf16[192,4,5,128]{3,0,2,1:T(8,128)(2,1)S(1)} fusion(f32[4,1024,192,5]{1,2,3,0:T(8,128)S(1)} %get-tuple-element.144, f32[192,4,5]{0,2,1:T(8,128)S(1)} %get-tuple-element.145, pred[1024]{0:T(1024)(128)(4,1)S(1)} %and.179, bf16[1024,4,128,1]{2,1,0,3:T(4,128)(2,1)S(1)} %bitcast.94, f32[192,4,5]{0,2,1:T(8,128)S(1)} %fusion.48), kind=kOutput, calls=%fused_computation.17.clone.1 | convolution fusion | flops 1023344640 | bytes 17792000 | tf_op jit(solution)/shard_map/while/body/eval_jaxpr/rkgt,tkd->rkgd/dot_general | solution.py:50
  257.7 1.3 constant_dynamic-slice_fusion.7
  259.6 1.7 copy_bitcast_fusion.2
  261.3 1.2 fusion.47
  262.5 1.3 squeeze.29
  263.8 1.1 squeeze.30
  265.0 2.9 %bitcast_reduce_fusion.2 = (f32[192,4,5]{0,2,1:T(8,128)S(1)}, f32[4,1024,192,5]{1,2,3,0:T(8,128)S(1)}) fusion(pred[1024]{0:T(1024)(128)(4,1)S(1)} %and.179, bf16[192,4,5,128]{0,3,2,1:T(8,128)(2,1)S(1)} %bitcast.91, bf16[1024,4,128,1]{2,1,0,3:T(4,128)(2,1)S(1)} %bitcast.93), kind=kOutput, calls=%fused_computation.8.clone.1 | convolution fusion | flops 1018425600 | bytes 17776640 | tf_op jit(solution)/shard_map/while/body/eval_jaxpr/rkgd,tkd->rkgt/dot_general | solution.py:37
  267.9 3.9 %fusion.48 = f32[192,4,5]{0,2,1:T(8,128)S(1)} fusion(f32[4,1024,192,5]{1,2,3,0:T(8,128)S(1)} %get-tuple-element.144, f32[192,4,5]{0,2,1:T(8,128)S(1)} %get-tuple-element.145, pred[1024]{0:T(1024)(128)(4,1)S(1)} %and.179), kind=kLoop, calls=%fused_computation.11.clone.1 | loop fusion | flops 15724800 | bytes 15760384 | tf_op jit(solution)/shard_map/while/body/eval_jaxpr/reduce_sum | solution.py:47
  271.9 3.9 %bitcast_divide_fusion.2 = bf16[192,4,5,128]{3,0,2,1:T(8,128)(2,1)S(1)} fusion(f32[4,1024,192,5]{1,2,3,0:T(8,128)S(1)} %get-tuple-element.144, f32[192,4,5]{0,2,1:T(8,128)S(1)} %get-tuple-element.145, pred[1024]{0:T(1024)(128)(4,1)S(1)} %and.179, bf16[1024,4,128,1]{2,1,0,3:T(4,128)(2,1)S(1)} %bitcast.94, f32[192,4,5]{0,2,1:T(8,128)S(1)} %fusion.48), kind=kOutput, calls=%fused_computation.17.clone.1 | convolution fusion | flops 1023344640 | bytes 17792000 | tf_op jit(solution)/shard_map/while/body/eval_jaxpr/rkgt,tkd->rkgd/dot_general | solution.py:50
  (97 shorter events, 28.6 us)
Async XLA Ops:
  6.5 10.1 %copy-start = (s32[64]{0:T(128)S(1)}, s32[64]{0:T(128)}, u32[]{:S(2)}) copy-start(s32[64]{0:T(128)} %param.16) | copy-start | bytes 772
  6.5 205.8 %all-gather.2.cloned.1.call-start = ((), (), s32[]{:S(2)}) async-start(), calls=%async_computation | async-start | bytes 27852800 | tf_op jit(solution)/shard_map/all_gather | solution.py:68
  7.3 14.2 %collective-permute-start.2 = (s32[2,2]{1,0:T(2,128)}, s32[2,2]{1,0:T(2,128)S(1)}, u32[]{:S(2)}, u32[]{:S(2)}) collective-permute-start(s32[2,2]{1,0:T(2,128)} %param.17), channel_id=1, source_target_pairs={{15,0},{0,1},{1,2},{2,3},{3,4},{4,5},{5,6},{6,7},{7,8},{8,9},{9,10... | collective-permute-start | bytes 56 | tf_op jit(solution)/shard_map/ppermute | solution.py:18
  7.8 14.5 %collective-permute-start = (s32[2,2]{1,0:T(2,128)}, s32[2,2]{1,0:T(2,128)S(1)}, u32[]{:S(2)}, u32[]{:S(2)}) collective-permute-start(s32[2,2]{1,0:T(2,128)} %param.17), channel_id=1, source_target_pairs={{14,0},{15,1},{0,2},{1,3},{2,4},{3,5},{4,6},{5,7},{6,8},{7,9},{8,1... | collective-permute-start | bytes 56 | tf_op jit(solution)/shard_map/ppermute | solution.py:18
  10.3 25.5 %collective-permute-start.4 = (s32[2,2]{1,0:T(2,128)}, s32[2,2]{1,0:T(2,128)S(1)}, u32[]{:S(2)}, u32[]{:S(2)}) collective-permute-start(s32[2,2]{1,0:T(2,128)} %param.17), channel_id=1, source_target_pairs={{1,0},{2,1},{3,2},{4,3},{5,4},{6,5},{7,6},{8,7},{9,8},{10,9},{11,1... | collective-permute-start | bytes 56 | tf_op jit(solution)/shard_map/ppermute | solution.py:18
  14.4 22.1 %collective-permute-start.6 = (s32[2,2]{1,0:T(2,128)}, s32[2,2]{1,0:T(2,128)S(1)}, u32[]{:S(2)}, u32[]{:S(2)}) collective-permute-start(s32[2,2]{1,0:T(2,128)} %param.17), channel_id=1, source_target_pairs={{2,0},{3,1},{4,2},{5,3},{6,4},{7,5},{8,6},{9,7},{10,8},{11,9},{12,... | collective-permute-start | bytes 56 | tf_op jit(solution)/shard_map/ppermute | solution.py:18
  33.1 48.2 %collective-permute-start.1 = (bf16[2,512,512]{2,1,0:T(8,128)(2,1)}, bf16[2,512,512]{2,1,0:T(8,128)(2,1)S(1)}, u32[]{:S(2)}, u32[]{:S(2)}) collective-permute-start(bf16[2,512,512]{2,1,0:T(8,128)(2,1)} %get-tuple-element.89), channel_id=1, source_target_pairs={{2,0},{3,1},{4,2},{5,3},{6,4},{7,5},{8,6},{9,7},{10,8},{11,9},{12,... | collective-permute-start | bytes 3145736 | tf_op jit(solution)/shard_map/ppermute | solution.py:18
  36.6 78.1 %collective-permute-start.3 = (bf16[2,512,512]{2,1,0:T(8,128)(2,1)S(1)}, bf16[2,512,512]{2,1,0:T(8,128)(2,1)S(1)}, u32[]{:S(2)}, u32[]{:S(2)}) collective-permute-start(bf16[2,512,512]{2,1,0:T(8,128)(2,1)S(1)} %get-tuple-element.88), channel_id=1, source_target_pairs={{1,0},{2,1},{3,2},{4,3},{5,4},{6,5},{7,6},{8,7},{9,8},{10,9},{11,1... | collective-permute-start | bytes 3145736 | tf_op jit(solution)/shard_map/ppermute | solution.py:18
  43.1 71.7 %copy-start.3 = (bf16[4,2,512,512]{3,2,1,0:T(8,128)(2,1)S(1)}, bf16[4,2,512,512]{3,2,1,0:T(8,128)(2,1)}, u32[]{:S(2)}) copy-start(bf16[4,2,512,512]{3,2,1,0:T(8,128)(2,1)} %param.15) | copy-start | bytes 12582916
  117.1 2.4 copy-start.4
  119.5 49.9 %collective-permute-start.5 = (bf16[2,512,512]{2,1,0:T(8,128)(2,1)S(1)}, bf16[2,512,512]{2,1,0:T(8,128)(2,1)S(1)}, u32[]{:S(2)}, u32[]{:S(2)}) collective-permute-start(bf16[2,512,512]{2,1,0:T(8,128)(2,1)S(1)} %get-tuple-element.87), channel_id=1, source_target_pairs={{15,0},{0,1},{1,2},{2,3},{3,4},{4,5},{5,6},{6,7},{7,8},{8,9},{9,10... | collective-permute-start | bytes 3145736 | tf_op jit(solution)/shard_map/ppermute | solution.py:18
  120.1 51.1 %collective-permute-start.7 = (bf16[2,512,512]{2,1,0:T(8,128)(2,1)S(1)}, bf16[2,512,512]{2,1,0:T(8,128)(2,1)S(1)}, u32[]{:S(2)}, u32[]{:S(2)}) collective-permute-start(bf16[2,512,512]{2,1,0:T(8,128)(2,1)S(1)} %get-tuple-element.85), channel_id=1, source_target_pairs={{14,0},{15,1},{0,2},{1,3},{2,4},{3,5},{4,6},{5,7},{6,8},{7,9},{8,1... | collective-permute-start | bytes 3145736 | tf_op jit(solution)/shard_map/ppermute | solution.py:18
  177.6 34.8 %copy-start.6 = (f32[5120]{0:T(1024)S(1)}, f32[5120]{0:T(1024)}, u32[]{:S(2)}) copy-start(f32[5120]{0:T(1024)} %param.12) | copy-start | bytes 61444
  177.6 34.8 %copy-start.7 = (f32[2560]{0:T(1024)S(1)}, f32[2560]{0:T(1024)}, u32[]{:S(2)}) copy-start(f32[2560]{0:T(1024)} %param.14) | copy-start | bytes 30724
  182.3 47.5 %copy-start.5 = (s32[2,2]{1,0:T(2,128)S(1)}, s32[2,2]{1,0:T(2,128)}, u32[]{:S(2)}) copy-start(s32[2,2]{1,0:T(2,128)} %param.17) | copy-start | bytes 52
  182.3 47.5 %copy-start.8 = (s32[2]{0:T(128)S(1)}, s32[2]{0:T(128)}, u32[]{:S(2)}) copy-start(s32[2]{0:T(128)} %param.19) | copy-start | bytes 28
  182.3 47.5 %copy-start.9 = (s32[2]{0:T(128)S(1)}, s32[2]{0:T(128)}, u32[]{:S(2)}) copy-start(s32[2]{0:T(128)} %param.18) | copy-start | bytes 28
  243.7 4.0 %copy-start.2 = (bf16[1024,4,128]{2,1,0:T(4,128)(2,1)S(1)}, bf16[1024,4,128]{2,1,0:T(4,128)(2,1)}, u32[]{:S(2)}) copy-start(bf16[1024,4,128]{2,1,0:T(4,128)(2,1)} %squeeze.30) | copy-start | bytes 3145732 | tf_op jit(solution)/shard_map/while
  267.9 4.0 %copy-start.2 = (bf16[1024,4,128]{2,1,0:T(4,128)(2,1)S(1)}, bf16[1024,4,128]{2,1,0:T(4,128)(2,1)}, u32[]{:S(2)}) copy-start(bf16[1024,4,128]{2,1,0:T(4,128)(2,1)} %squeeze.30) | copy-start | bytes 3145732 | tf_op jit(solution)/shard_map/while
  278.3 0.7 copy-start.1
Sparse Core Ops, SparseCore 0:
  9.0 203.3 all-gather.1
where the time goes:
time: 287 us; the launch traced here: 286 us
  waiting for transfers between devices  148 us (52%)
  local copies, waits for them, and re-layouts  37.2 us (13%)
  other arithmetic  31.4 us (11%)
  matrix products  31.2 us (11%)
  between operations  23.2 us (8%)
  starting transfers between devices  12.4 us (4%)
    ppermute x8, waiting for transfers between devices, passed_along(): return lax.ppermute(block, axis, route)  117 us
    all_gather x1, waiting for transfers between devices, shards(): whole_weight = lax.all_gather(q_weight, 'blk', axis=0, tiled=True)  30 us
    dot_general x1, matrix products, shards(): jnp.dot(normed, whole_weight, preferred_element_type=jnp.float32)  17.5 us
    ppermute x8, starting transfers between devices, passed_along(): return lax.ppermute(block, axis, route)  12.3 us
    reduce_sum x2, other arithmetic, attend_single(): denominator = jnp.sum(exponent, axis=-1)  7.9 us
    dot_general x2, matrix products, attend_single(): jnp.einsum('rkgt,tkd->rkgd', weights, block_value_rows, preferred_element...  7.83 us
    select_n x2, other arithmetic, select_block(): return jnp.where(has_block, chosen, empty_block)  6.33 us
    dynamic_slice x8, local copies, waits for them, and re-layouts, attend_all(): lax.map(attend_single, (shaped, sketch_blocks, block_lists, hole_starts,...  6.01 us
  transfers between devices with their start and end apart: 9, of which 5 were waited for; matrix products, arithmetic and copies ran while one was open for 12% of the time, Pallas kernels for 0%

commit v1 on v0

--- a/solution.py
+++ b/solution.py
@@ -10,6 +10,27 @@
 BLOCK_TOKENS = 512
 BLOCKS_NEEDED = 2
 REACH = 2
+
+
+def gather_around(array, axis, dim):
+    size, index, extent = (lax.axis_size(axis), lax.axis_index(axis), array.shape[dim])
+    ahead = [(i, (i + 1) % size) for i in range(size)]
+    behind = [(i, (i - 1) % size) for i in range(size)]
+    out = jnp.zeros((*array.shape[:dim], size * extent, *array.shape[dim + 1 :]), array.dtype)
+    out = lax.dynamic_update_slice_in_dim(out, array, index * extent, axis=dim)
+    from_left = from_right = array
+    half = size // 2
+    for lap in range(1, half + 1):
+        from_left = lax.ppermute(from_left, axis, ahead)
+        out = lax.dynamic_update_slice_in_dim(
+            out, from_left, (index - lap) % size * extent, axis=dim
+        )
+        if lap < size - half:
+            from_right = lax.ppermute(from_right, axis, behind)
+            out = lax.dynamic_update_slice_in_dim(
+                out, from_right, (index + lap) % size * extent, axis=dim
+            )
+    return out
 
 
 def passed_along(block, axis, distance):
@@ -65,7 +86,7 @@
 
 def shards(hidden, norm_gain, q_weight, q_bias, kv_store, block_home, need_ids, hole_pos, fill_len):
     normed = rms_normed(hidden, norm_gain)
-    whole_weight = lax.all_gather(q_weight, "blk", axis=0, tiled=True)
+    whole_weight = gather_around(q_weight, "blk", 0)
     projected = jnp.dot(normed, whole_weight, preferred_element_type=jnp.float32)
     query = (projected + q_bias).astype(jnp.bfloat16)
     device_count = lax.axis_size("blk")

time: 287 us -> 430 us (1.50)
  the two profiles are of different devices: /device:TPU:0 before, /device:TPU:1 now
where the time goes in v1:
time: 430 us; the launch traced here: 429 us
  waiting for transfers between devices  239 us (56%)
  local copies, waits for them, and re-layouts  82.3 us (19%)
  matrix products  36.5 us (8%)
  other arithmetic  33.4 us (8%)
  starting transfers between devices  25.2 us (6%)
  between operations  9.85 us (2%)
    ppermute x8, waiting for transfers between devices, gather_around(): from_left = lax.ppermute(from_left, axis, ahead)  116 us
    ppermute x7, waiting for transfers between devices, gather_around(): from_right = lax.ppermute(from_right, axis, behind)  108 us
    ppermute x8, starting transfers between devices, gather_around(): from_left = lax.ppermute(from_left, axis, ahead)  16.6 us
    dynamic_update_slice x8, local copies, waits for them, and re-layouts, gather_around(): lax.dynamic_update_slice_in_dim(out, from_left, (index - lap) % size * ex...  16.1 us
    dot_general x1, matrix products, shards(): jnp.dot(normed, whole_weight, preferred_element_type=jnp.float32)  15.6 us
    dot_general x2, matrix products, attend_single(): jnp.einsum('rkgt,tkd->rkgd', weights, block_value_rows, preferred_element...  15 us
    dynamic_update_slice x7, local copies, waits for them, and re-layouts, gather_around(): lax.dynamic_update_slice_in_dim(out, from_right, (index + lap) % size * e...  14.9 us
    ppermute x8, waiting for transfers between devices, passed_along(): return lax.ppermute(block, axis, route)  14.6 us
  transfers between devices with their start and end apart: 23, of which 14 were waited for; matrix products, arithmetic and copies ran while one was open for 19% of the time, Pallas kernels for 0%

profile of v1, /device:TPU:1, one launch (start us, length us, event | category | flops | bytes accessed | tf_op | source)
XLA Modules:
  0.0 428.6 jit_solution(3161124584141743834)
XLA Ops:
  2.6 35.9 %collective-permute-done.8 = bf16[320,2560]{1,0:T(8,128)(2,1)} collective-permute-done((bf16[320,2560]{1,0:T(8,128)(2,1)}, bf16[320,2560]{1,0:T(8,128)(2,1)}, u32[]{:S(2)}, u32[]{:S(2)}) %collective-permute-start.8) | collective-permute-done | bytes 1638432 | tf_op jit(solution)/shard_map/ppermute | solution.py:24
  44.7 13.8 %collective-permute-done.9 = bf16[320,2560]{1,0:T(8,128)(2,1)S(1)} collective-permute-done((bf16[320,2560]{1,0:T(8,128)(2,1)}, bf16[320,2560]{1,0:T(8,128)(2,1)S(1)}, u32[]{:S(2)}, u32[]{:S(2)}) %collective-permute-start.9) | collective-permute-done | bytes 1638432 | tf_op jit(solution)/shard_map/ppermute | solution.py:29
  59.2 17.8 %collective-permute-done.10 = bf16[320,2560]{1,0:T(8,128)(2,1)S(1)} collective-permute-done((bf16[320,2560]{1,0:T(8,128)(2,1)}, bf16[320,2560]{1,0:T(8,128)(2,1)S(1)}, u32[]{:S(2)}, u32[]{:S(2)}) %collective-permute-start.10) | collective-permute-done | bytes 1638432 | tf_op jit(solution)/shard_map/ppermute | solution.py:24
  82.2 3.0 fusion.15
  85.1 8.8 %broadcast_in_dim.73 = bf16[5120,2560]{1,0:T(8,128)(2,1)} broadcast(bf16[]{:T(256)} %constant.238.clone.1), dimensions={} | broadcast | bytes 26214402 | tf_op jit(solution)/shard_map/broadcast_in_dim | solution.py:19
  106.0 4.3 %select_bitcast_fusion.2 = (bf16[2,512,512]{2,1,0:T(8,128)(2,1)}, bf16[2,512,512]{2,1,0:T(8,128)(2,1)}) fusion(bf16[4,2,512,512]{3,2,1,0:T(8,128)(2,1)} %param.15, s32[]{:T(128)S(6)} %select_n.367, pred[]{:T(512)} %get-tuple-element.77, s32[]{:T(128)S(6)} %select_n.359, pred[]{:T(512)} %get-tuple-element.92), kind=kLoop, calls=%fused_computation.48 | loop fusion | flops 1048576 | bytes 4194314 | tf_op jit(solution)/shard_map/jit(_where)/select_n | solution.py:103
  110.4 5.5 %collective-permute-start.1 = (bf16[2,512,512]{2,1,0:T(8,128)(2,1)}, bf16[2,512,512]{2,1,0:T(8,128)(2,1)}, u32[]{:S(2)}, u32[]{:S(2)}) collective-permute-start(bf16[2,512,512]{2,1,0:T(8,128)(2,1)} %get-tuple-element.89), channel_id=1, source_target_pairs={{2,0},{3,1},{4,2},{5,3},{6,4},{7,5},{8,6},{9,7},{10,8},{11,9},{12,... | collective-permute-start | bytes 3145736 | tf_op jit(solution)/shard_map/ppermute | solution.py:39
  118.1 27.5 %collective-permute-done.13 = bf16[320,2560]{1,0:T(8,128)(2,1)} collective-permute-done((bf16[320,2560]{1,0:T(8,128)(2,1)}, bf16[320,2560]{1,0:T(8,128)(2,1)}, u32[]{:S(2)}, u32[]{:S(2)}) %collective-permute-start.13) | collective-permute-done | bytes 1638432 | tf_op jit(solution)/shard_map/ppermute | solution.py:29
  150.5 35.1 %collective-permute-done.14 = bf16[320,2560]{1,0:T(8,128)(2,1)} collective-permute-done((bf16[320,2560]{1,0:T(8,128)(2,1)}, bf16[320,2560]{1,0:T(8,128)(2,1)}, u32[]{:S(2)}, u32[]{:S(2)}) %collective-permute-start.14) | collective-permute-done | bytes 1638432 | tf_op jit(solution)/shard_map/ppermute | solution.py:24
  192.6 3.8 select_bitcast_fusion
  199.6 38.1 %collective-permute-done.15 = bf16[320,2560]{1,0:T(8,128)(2,1)} collective-permute-done((bf16[320,2560]{1,0:T(8,128)(2,1)}, bf16[320,2560]{1,0:T(8,128)(2,1)}, u32[]{:S(2)}, u32[]{:S(2)}) %collective-permute-start.15) | collective-permute-done | bytes 1638432 | tf_op jit(solution)/shard_map/ppermute | solution.py:29
  240.7 5.7 %collective-permute-done.5 = bf16[2,512,512]{2,1,0:T(8,128)(2,1)} collective-permute-done((bf16[2,512,512]{2,1,0:T(8,128)(2,1)}, bf16[2,512,512]{2,1,0:T(8,128)(2,1)}, u32[]{:S(2)}, u32[]{:S(2)}) %collective-permute-start.5) | collective-permute-done | bytes 1048608 | tf_op jit(solution)/shard_map/ppermute | solution.py:39
  248.8 8.9 %collective-permute-done.7 = bf16[2,512,512]{2,1,0:T(8,128)(2,1)S(1)} collective-permute-done((bf16[2,512,512]{2,1,0:T(8,128)(2,1)}, bf16[2,512,512]{2,1,0:T(8,128)(2,1)S(1)}, u32[]{:S(2)}, u32[]{:S(2)}) %collective-permute-start.7) | collective-permute-done | bytes 1048608 | tf_op jit(solution)/shard_map/ppermute | solution.py:39
  258.7 5.3 %gather_fusion.6 = bf16[4,2,512,512]{3,2,1,0:T(8,128)(2,1)} fusion(bf16[5,2,512,512]{3,2,1,0:T(8,128)(2,1)} %bitcast_dynamic-update-slice_fusion, s32[1024]{0:T(1024)S(1)} %pad_clamp_fusion), kind=kCustom, calls=%fused_computation.6 | custom fusion | bytes 8388624 | tf_op jit(solution)/shard_map/jit(_take)/gather | solution.py:115
  264.0 4.7 %broadcast_select_fusion = bf16[2,2,2,512,512]{4,3,2,1,0:T(8,128)(2,1)} fusion(bf16[2,2,2,512,512]{4,3,2,1,0:T(8,128)(2,1)} %bitcast.95, pred[2,2]{1,0:T(4,128)(4,1)S(1)} %compare_and_fusion.1), kind=kLoop, calls=%fused_computation.38 | loop fusion | flops 2097152 | bytes 8388612 | tf_op jit(solution)/shard_map/jit(_take)/select_n | solution.py:115
  270.1 6.0 %collective-permute-done.17 = bf16[320,2560]{1,0:T(8,128)(2,1)} collective-permute-done((bf16[320,2560]{1,0:T(8,128)(2,1)}, bf16[320,2560]{1,0:T(8,128)(2,1)}, u32[]{:S(2)}, u32[]{:S(2)}) %collective-permute-start.17) | collective-permute-done | bytes 1638432 | tf_op jit(solution)/shard_map/ppermute | solution.py:29
  276.1 2.8 constant_dynamic-update-slice_fusion.12
  278.8 14.0 %collective-permute-done.18 = bf16[320,2560]{1,0:T(8,128)(2,1)S(1)} collective-permute-done((bf16[320,2560]{1,0:T(8,128)(2,1)}, bf16[320,2560]{1,0:T(8,128)(2,1)S(1)}, u32[]{:S(2)}, u32[]{:S(2)}) %collective-permute-start.18) | collective-permute-done | bytes 1638432 | tf_op jit(solution)/shard_map/ppermute | solution.py:24
  300.6 2.7 constant_dynamic-update-slice_fusion.9
  303.3 2.8 constant_dynamic-update-slice_fusion.8
  306.1 8.3 %collective-permute-done.19 = bf16[320,2560]{1,0:T(8,128)(2,1)S(1)} collective-permute-done((bf16[320,2560]{1,0:T(8,128)(2,1)}, bf16[320,2560]{1,0:T(8,128)(2,1)S(1)}, u32[]{:S(2)}, u32[]{:S(2)}) %collective-permute-start.19) | collective-permute-done | bytes 1638432 | tf_op jit(solution)/shard_map/ppermute | solution.py:29
  317.1 13.7 %collective-permute-done.20 = bf16[320,2560]{1,0:T(8,128)(2,1)S(1)} collective-permute-done((bf16[320,2560]{1,0:T(8,128)(2,1)S(1)}, bf16[320,2560]{1,0:T(8,128)(2,1)S(1)}, u32[]{:S(2)}, u32[]{:S(2)}) %collective-permute-start.20) | collective-permute-done | bytes 1638432 | tf_op jit(solution)/shard_map/ppermute | solution.py:24
  333.3 2.7 constant_dynamic-update-slice_fusion.6
  339.9 12.6 %collective-permute-done.21 = bf16[320,2560]{1,0:T(8,128)(2,1)S(1)} collective-permute-done((bf16[320,2560]{1,0:T(8,128)(2,1)S(1)}, bf16[320,2560]{1,0:T(8,128)(2,1)S(1)}, u32[]{:S(2)}, u32[]{:S(2)}) %collective-permute-start.21) | collective-permute-done | bytes 1638432 | tf_op jit(solution)/shard_map/ppermute | solution.py:29
  355.1 15.6 %fusion.18 = bf16[384,2560]{1,0:T(8,128)(2,1)} fusion(bf16[5120,2560]{1,0:T(8,128)(2,1)} %constant_dynamic-update-slice_fusion.1, bf16[384,5120]{1,0:T(8,128)(2,1)S(1)} %copy-done.4, f32[5120]{0:T(1024)S(1)} %copy-done.7, f32[384]{0:T(512)S(1)} %add_rsqrt_fusion, f32[2560]{0:T(1024)S(1)} %copy-done.8), kind=kOutput, calls=%fused_computation.37 | convolution fusion | flops 10076160000 | bytes 32144896 | tf_op jit(solution)/shard_map/dot_general | solution.py:90
  370.7 57.3 %while.10 = (s32[]{:T(128)}, bf16[2,192,2560]{2,1,0:T(8,128)(2,1)}, s32[2]{0:T(128)S(1)}, bf16[2,2,2,512,512]{4,3,2,1,0:T(8,128)(2,1)}, s32[2,2]{1,0:T(2,128)S(1...) while((s32[]{:T(128)}, bf16[2,192,2560]{2,1,0:T(8,128)(2,1)}, s32[2]{0:T(128)S(1)}, ...), condition=%wide.region_14.15_spmd, body=%wide.region_11.14_spmd.sunk | while | flops 2057990912 | bytes 138627664 | solution.py:83
  379.9 3.0 bitcast_reduce_fusion.2
  382.9 4.1 fusion.48
  388.7 7.5 %bitcast_divide_fusion.2 = bf16[192,4,5,128]{3,0,2,1:T(8,128)(2,1)S(1)} fusion(f32[4,1024,192,5]{1,2,3,0:T(8,128)} %copy-done.2, f32[192,4,5]{0,2,1:T(8,128)S(1)} %get-tuple-element.145, pred[1024]{0:T(1024)(128)(4,1)S(1)} %and.255, bf16[1024,4,128,1]{2,1,0,3:T(4,128)(2,1)S(1)} %bitcast.94, f32[192,4,5]{0,2,1:T(8,128)S(1)} %fusion.48), kind=kOutput, calls=%fused_computation.17.clone.1 | convolution fusion | flops 1023344640 | bytes 17792000 | tf_op jit(solution)/shard_map/while/body/eval_jaxpr/rkgt,tkd->rkgd/dot_general | solution.py:71
  408.6 3.0 bitcast_reduce_fusion.2
  411.5 4.1 fusion.48
  417.3 7.5 %bitcast_divide_fusion.2 = bf16[192,4,5,128]{3,0,2,1:T(8,128)(2,1)S(1)} fusion(f32[4,1024,192,5]{1,2,3,0:T(8,128)} %copy-done.2, f32[192,4,5]{0,2,1:T(8,128)S(1)} %get-tuple-element.145, pred[1024]{0:T(1024)(128)(4,1)S(1)} %and.255, bf16[1024,4,128,1]{2,1,0,3:T(4,128)(2,1)S(1)} %bitcast.94, f32[192,4,5]{0,2,1:T(8,128)S(1)} %fusion.48), kind=kOutput, calls=%fused_computation.17.clone.1 | convolution fusion | flops 1023344640 | bytes 17792000 | tf_op jit(solution)/shard_map/while/body/eval_jaxpr/rkgt,tkd->rkgd/dot_general | solution.py:71
  (143 shorter events, 87.7 us)
Async XLA Ops:
  0.0 43.3 %copy-start = (s32[64]{0:T(128)S(1)}, s32[64]{0:T(128)}, u32[]{:S(2)}) copy-start(s32[64]{0:T(128)} %param.16) | copy-start | bytes 772
  0.0 38.6 %collective-permute-start.8 = (bf16[320,2560]{1,0:T(8,128)(2,1)}, bf16[320,2560]{1,0:T(8,128)(2,1)}, u32[]{:S(2)}, u32[]{:S(2)}) collective-permute-start(bf16[320,2560]{1,0:T(8,128)(2,1)} %param.13), channel_id=1, source_target_pairs={{0,1},{1,2},{2,3},{3,4},{4,5},{5,6},{6,7},{7,8},{8,9},{9,10},{10,1... | collective-permute-start | bytes 4915208 | tf_op jit(solution)/shard_map/ppermute | solution.py:24
  2.6 55.9 %collective-permute-start.9 = (bf16[320,2560]{1,0:T(8,128)(2,1)}, bf16[320,2560]{1,0:T(8,128)(2,1)S(1)}, u32[]{:S(2)}, u32[]{:S(2)}) collective-permute-start(bf16[320,2560]{1,0:T(8,128)(2,1)} %param.13), channel_id=1, source_target_pairs={{0,15},{1,0},{2,1},{3,2},{4,3},{5,4},{6,5},{7,6},{8,7},{9,8},{10,9... | collective-permute-start | bytes 4915208 | tf_op jit(solution)/shard_map/ppermute | solution.py:29
  38.6 38.4 %collective-permute-start.10 = (bf16[320,2560]{1,0:T(8,128)(2,1)}, bf16[320,2560]{1,0:T(8,128)(2,1)S(1)}, u32[]{:S(2)}, u32[]{:S(2)}) collective-permute-start(bf16[320,2560]{1,0:T(8,128)(2,1)} %collective-permute-done.8), channel_id=1, source_target_pairs={{0,1},{1,2},{2,3},{3,4},{4,5},{5,6},{6,7},{7,8},{8,9},{9,10},{10,1... | collective-permute-start | bytes 4915208 | tf_op jit(solution)/shard_map/ppermute | solution.py:24
  41.0 54.1 %collective-permute-start = (s32[2,2]{1,0:T(2,128)}, s32[2,2]{1,0:T(2,128)S(1)}, u32[]{:S(2)}, u32[]{:S(2)}) collective-permute-start(s32[2,2]{1,0:T(2,128)} %param.17), channel_id=1, source_target_pairs={{14,0},{15,1},{0,2},{1,3},{2,4},{3,5},{4,6},{5,7},{6,8},{7,9},{8,1... | collective-permute-start | bytes 56 | tf_op jit(solution)/shard_map/ppermute | solution.py:39
  41.1 54.2 %collective-permute-start.2 = (s32[2,2]{1,0:T(2,128)}, s32[2,2]{1,0:T(2,128)S(1)}, u32[]{:S(2)}, u32[]{:S(2)}) collective-permute-start(s32[2,2]{1,0:T(2,128)} %param.17), channel_id=1, source_target_pairs={{15,0},{0,1},{1,2},{2,3},{3,4},{4,5},{5,6},{6,7},{7,8},{8,9},{9,10... | collective-permute-start | bytes 56 | tf_op jit(solution)/shard_map/ppermute | solution.py:39
  41.7 74.2 %collective-permute-start.4 = (s32[2,2]{1,0:T(2,128)}, s32[2,2]{1,0:T(2,128)S(1)}, u32[]{:S(2)}, u32[]{:S(2)}) collective-permute-start(s32[2,2]{1,0:T(2,128)} %param.17), channel_id=1, source_target_pairs={{1,0},{2,1},{3,2},{4,3},{5,4},{6,5},{7,6},{8,7},{9,8},{10,9},{11,1... | collective-permute-start | bytes 56 | tf_op jit(solution)/shard_map/ppermute | solution.py:39
  58.5 38.2 %collective-permute-start.11 = (bf16[320,2560]{1,0:T(8,128)(2,1)S(1)}, bf16[320,2560]{1,0:T(8,128)(2,1)}, u32[]{:S(2)}, u32[]{:S(2)}) collective-permute-start(bf16[320,2560]{1,0:T(8,128)(2,1)S(1)} %collective-permute-done.9), channel_id=1, source_target_pairs={{0,15},{1,0},{2,1},{3,2},{4,3},{5,4},{6,5},{7,6},{8,7},{9,8},{10,9... | collective-permute-start | bytes 4915208 | tf_op jit(solution)/shard_map/ppermute | solution.py:29
  77.0 23.1 %collective-permute-start.12 = (bf16[320,2560]{1,0:T(8,128)(2,1)S(1)}, bf16[320,2560]{1,0:T(8,128)(2,1)}, u32[]{:S(2)}, u32[]{:S(2)}) collective-permute-start(bf16[320,2560]{1,0:T(8,128)(2,1)S(1)} %collective-permute-done.10), channel_id=1, source_target_pairs={{0,1},{1,2},{2,3},{3,4},{4,5},{5,6},{6,7},{7,8},{8,9},{9,10},{10,1... | collective-permute-start | bytes 4915208 | tf_op jit(solution)/shard_map/ppermute | solution.py:24
  85.1 8.8 %copy-start.5 = (bf16[320,2560]{1,0:T(8,128)(2,1)S(1)}, bf16[320,2560]{1,0:T(8,128)(2,1)}, u32[]{:S(2)}) copy-start(bf16[320,2560]{1,0:T(8,128)(2,1)} %param.13) | copy-start | bytes 4915204
  85.1 10.1 %copy-start.6 = (s32[2,2]{1,0:T(2,128)S(1)}, s32[2,2]{1,0:T(2,128)}, u32[]{:S(2)}) copy-start(s32[2,2]{1,0:T(2,128)} %param.17) | copy-start | bytes 52
  95.2 21.5 %collective-permute-start.6 = (s32[2,2]{1,0:T(2,128)S(1)}, s32[2,2]{1,0:T(2,128)S(1)}, u32[]{:S(2)}, u32[]{:S(2)}) collective-permute-start(s32[2,2]{1,0:T(2,128)S(1)} %copy-done.6), channel_id=1, source_target_pairs={{2,0},{3,1},{4,2},{5,3},{6,4},{7,5},{8,6},{9,7},{10,8},{11,9},{12,... | collective-permute-start | bytes 56 | tf_op jit(solution)/shard_map/ppermute | solution.py:39
  96.7 48.8 %collective-permute-start.13 = (bf16[320,2560]{1,0:T(8,128)(2,1)}, bf16[320,2560]{1,0:T(8,128)(2,1)}, u32[]{:S(2)}, u32[]{:S(2)}) collective-permute-start(bf16[320,2560]{1,0:T(8,128)(2,1)} %collective-permute-done.11), channel_id=1, source_target_pairs={{0,15},{1,0},{2,1},{3,2},{4,3},{5,4},{6,5},{7,6},{8,7},{9,8},{10,9... | collective-permute-start | bytes 4915208 | tf_op jit(solution)/shard_map/ppermute | solution.py:29
  100.1 85.4 %collective-permute-start.14 = (bf16[320,2560]{1,0:T(8,128)(2,1)}, bf16[320,2560]{1,0:T(8,128)(2,1)}, u32[]{:S(2)}, u32[]{:S(2)}) collective-permute-start(bf16[320,2560]{1,0:T(8,128)(2,1)} %collective-permute-done.12), channel_id=1, source_target_pairs={{0,1},{1,2},{2,3},{3,4},{4,5},{5,6},{6,7},{7,8},{8,9},{9,10},{10,1... | collective-permute-start | bytes 4915208 | tf_op jit(solution)/shard_map/ppermute | solution.py:24
  110.4 77.7 %collective-permute-start.1 = (bf16[2,512,512]{2,1,0:T(8,128)(2,1)}, bf16[2,512,512]{2,1,0:T(8,128)(2,1)}, u32[]{:S(2)}, u32[]{:S(2)}) collective-permute-start(bf16[2,512,512]{2,1,0:T(8,128)(2,1)} %get-tuple-element.89), channel_id=1, source_target_pairs={{2,0},{3,1},{4,2},{5,3},{6,4},{7,5},{8,6},{9,7},{10,8},{11,9},{12,... | collective-permute-start | bytes 3145736 | tf_op jit(solution)/shard_map/ppermute | solution.py:39
  115.9 74.4 %collective-permute-start.3 = (bf16[2,512,512]{2,1,0:T(8,128)(2,1)}, bf16[2,512,512]{2,1,0:T(8,128)(2,1)}, u32[]{:S(2)}, u32[]{:S(2)}) collective-permute-start(bf16[2,512,512]{2,1,0:T(8,128)(2,1)} %get-tuple-element.88), channel_id=1, source_target_pairs={{1,0},{2,1},{3,2},{4,3},{5,4},{6,5},{7,6},{8,7},{9,8},{10,9},{11,1... | collective-permute-start | bytes 3145736 | tf_op jit(solution)/shard_map/ppermute | solution.py:39
  145.6 92.1 %collective-permute-start.15 = (bf16[320,2560]{1,0:T(8,128)(2,1)}, bf16[320,2560]{1,0:T(8,128)(2,1)}, u32[]{:S(2)}, u32[]{:S(2)}) collective-permute-start(bf16[320,2560]{1,0:T(8,128)(2,1)} %collective-permute-done.13), channel_id=1, source_target_pairs={{0,15},{1,0},{2,1},{3,2},{4,3},{5,4},{6,5},{7,6},{8,7},{9,8},{10,9... | collective-permute-start | bytes 4915208 | tf_op jit(solution)/shard_map/ppermute | solution.py:29
  150.5 42.1 %copy-start.3 = (bf16[4,2,512,512]{3,2,1,0:T(8,128)(2,1)S(1)}, bf16[4,2,512,512]{3,2,1,0:T(8,128)(2,1)}, u32[]{:S(2)}) copy-start(bf16[4,2,512,512]{3,2,1,0:T(8,128)(2,1)} %param.15) | copy-start | bytes 12582916
  185.6 53.4 %collective-permute-start.16 = (bf16[320,2560]{1,0:T(8,128)(2,1)}, bf16[320,2560]{1,0:T(8,128)(2,1)}, u32[]{:S(2)}, u32[]{:S(2)}) collective-permute-start(bf16[320,2560]{1,0:T(8,128)(2,1)} %collective-permute-done.14), channel_id=1, source_target_pairs={{0,1},{1,2},{2,3},{3,4},{4,5},{5,6},{6,7},{7,8},{8,9},{9,10},{10,1... | collective-permute-start | bytes 4915208 | tf_op jit(solution)/shard_map/ppermute | solution.py:24
  196.3 50.1 %collective-permute-start.5 = (bf16[2,512,512]{2,1,0:T(8,128)(2,1)}, bf16[2,512,512]{2,1,0:T(8,128)(2,1)}, u32[]{:S(2)}, u32[]{:S(2)}) collective-permute-start(bf16[2,512,512]{2,1,0:T(8,128)(2,1)} %get-tuple-element.87), channel_id=1, source_target_pairs={{15,0},{0,1},{1,2},{2,3},{3,4},{4,5},{5,6},{6,7},{7,8},{8,9},{9,10... | collective-permute-start | bytes 3145736 | tf_op jit(solution)/shard_map/ppermute | solution.py:39
  196.7 61.0 %collective-permute-start.7 = (bf16[2,512,512]{2,1,0:T(8,128)(2,1)}, bf16[2,512,512]{2,1,0:T(8,128)(2,1)S(1)}, u32[]{:S(2)}, u32[]{:S(2)}) collective-permute-start(bf16[2,512,512]{2,1,0:T(8,128)(2,1)} %get-tuple-element.85), channel_id=1, source_target_pairs={{14,0},{15,1},{0,2},{1,3},{2,4},{3,5},{4,6},{5,7},{6,8},{7,9},{8,1... | collective-permute-start | bytes 3145736 | tf_op jit(solution)/shard_map/ppermute | solution.py:39
  237.7 38.4 %collective-permute-start.17 = (bf16[320,2560]{1,0:T(8,128)(2,1)}, bf16[320,2560]{1,0:T(8,128)(2,1)}, u32[]{:S(2)}, u32[]{:S(2)}) collective-permute-start(bf16[320,2560]{1,0:T(8,128)(2,1)} %collective-permute-done.15), channel_id=1, source_target_pairs={{0,15},{1,0},{2,1},{3,2},{4,3},{5,4},{6,5},{7,6},{8,7},{9,8},{10,9... | collective-permute-start | bytes 4915208 | tf_op jit(solution)/shard_map/ppermute | solution.py:29
  239.0 53.8 %collective-permute-start.18 = (bf16[320,2560]{1,0:T(8,128)(2,1)}, bf16[320,2560]{1,0:T(8,128)(2,1)S(1)}, u32[]{:S(2)}, u32[]{:S(2)}) collective-permute-start(bf16[320,2560]{1,0:T(8,128)(2,1)} %collective-permute-done.16), channel_id=1, source_target_pairs={{0,1},{1,2},{2,3},{3,4},{4,5},{5,6},{6,7},{7,8},{8,9},{9,10},{10,1... | collective-permute-start | bytes 4915208 | tf_op jit(solution)/shard_map/ppermute | solution.py:24
  276.1 38.3 %collective-permute-start.19 = (bf16[320,2560]{1,0:T(8,128)(2,1)}, bf16[320,2560]{1,0:T(8,128)(2,1)S(1)}, u32[]{:S(2)}, u32[]{:S(2)}) collective-permute-start(bf16[320,2560]{1,0:T(8,128)(2,1)} %collective-permute-done.17), channel_id=1, source_target_pairs={{0,15},{1,0},{2,1},{3,2},{4,3},{5,4},{6,5},{7,6},{8,7},{9,8},{10,9... | collective-permute-start | bytes 4915208 | tf_op jit(solution)/shard_map/ppermute | solution.py:29
  292.8 38.0 %collective-permute-start.20 = (bf16[320,2560]{1,0:T(8,128)(2,1)S(1)}, bf16[320,2560]{1,0:T(8,128)(2,1)S(1)}, u32[]{:S(2)}, u32[]{:S(2)}) collective-permute-start(bf16[320,2560]{1,0:T(8,128)(2,1)S(1)} %collective-permute-done.18), channel_id=1, source_target_pairs={{0,1},{1,2},{2,3},{3,4},{4,5},{5,6},{6,7},{7,8},{8,9},{9,10},{10,1... | collective-permute-start | bytes 4915208 | tf_op jit(solution)/shard_map/ppermute | solution.py:24
  314.4 38.1 %collective-permute-start.21 = (bf16[320,2560]{1,0:T(8,128)(2,1)S(1)}, bf16[320,2560]{1,0:T(8,128)(2,1)S(1)}, u32[]{:S(2)}, u32[]{:S(2)}) collective-permute-start(bf16[320,2560]{1,0:T(8,128)(2,1)S(1)} %collective-permute-done.19), channel_id=1, source_target_pairs={{0,15},{1,0},{2,1},{3,2},{4,3},{5,4},{6,5},{7,6},{8,7},{9,8},{10,9... | collective-permute-start | bytes 4915208 | tf_op jit(solution)/shard_map/ppermute | solution.py:29
  330.8 23.0 %collective-permute-start.22 = (bf16[320,2560]{1,0:T(8,128)(2,1)S(1)}, bf16[320,2560]{1,0:T(8,128)(2,1)S(1)}, u32[]{:S(2)}, u32[]{:S(2)}) collective-permute-start(bf16[320,2560]{1,0:T(8,128)(2,1)S(1)} %collective-permute-done.20), channel_id=1, source_target_pairs={{0,1},{1,2},{2,3},{3,4},{4,5},{5,6},{6,7},{7,8},{8,9},{9,10},{10,1... | collective-permute-start | bytes 4915208 | tf_op jit(solution)/shard_map/ppermute | solution.py:24
  338.6 16.5 %copy-start.4 = (bf16[384,5120]{1,0:T(8,128)(2,1)S(1)}, bf16[384,5120]{1,0:T(8,128)(2,1)}, u32[]{:S(2)}) copy-start(bf16[384,5120]{1,0:T(8,128)(2,1)} %param.11) | copy-start | bytes 11796484
  338.6 16.5 %copy-start.7 = (f32[5120]{0:T(1024)S(1)}, f32[5120]{0:T(1024)}, u32[]{:S(2)}) copy-start(f32[5120]{0:T(1024)} %param.12) | copy-start | bytes 61444
  338.6 16.5 %copy-start.8 = (f32[2560]{0:T(1024)S(1)}, f32[2560]{0:T(1024)}, u32[]{:S(2)}) copy-start(f32[2560]{0:T(1024)} %param.14) | copy-start | bytes 30724
  355.1 15.6 %copy-start.9 = (s32[2]{0:T(128)S(1)}, s32[2]{0:T(128)}, u32[]{:S(2)}) copy-start(s32[2]{0:T(128)} %param.19) | copy-start | bytes 28
  355.1 15.6 %copy-start.10 = (s32[2]{0:T(128)S(1)}, s32[2]{0:T(128)}, u32[]{:S(2)}) copy-start(s32[2]{0:T(128)} %param.18) | copy-start | bytes 28
  (3 other events, 11.7 us)
